TPU v7x, 32 devices: a whole 2x2x4 slice. The times are simulated.
32 devices in a mesh: dp: 2 (over y), ctx: 4 (over x, core), head: 4 (over z).
Axes of the slice: x: 2, y: 2, z: 4, core: 2. Of those that a mesh axis runs over, the one named last changes fastest.
Arguments:
- mix_query: bfloat16 [4096, 8192], P(('dp', 'ctx', 'head')), parts along dimension 0, may hold values from -6 to 6
- mix_key: bfloat16 [4096, 8192], P(('dp', 'ctx', 'head')), parts along dimension 0, may hold values from -6 to 6
- mix_value: bfloat16 [4096, 8192], P(('dp', 'ctx', 'head')), parts along dimension 0, may hold values from -6 to 6
- mr_filter: bfloat16 [512, 128], replicated, may hold values from -0.5 to 0.5
- doc_ids: int32 [4096], P('dp'), parts along dimension 0, may hold values from 0 to 3, never falling along the last dimension, each value on 1 to 1536 neighbouring positions
- att_query: bfloat16 [4096, 4096], P(('dp', 'ctx'), 'head'), parts along dimension 0, may hold values from -5 to 5
- att_key: bfloat16 [4096, 4096], P(('dp', 'ctx'), 'head'), parts along dimension 0, may hold values from -5 to 5
- att_value: bfloat16 [4096, 4096], P(('dp', 'ctx'), 'head'), parts along dimension 0, may hold values from -6 to 6
Outputs:
- mixed: bfloat16 [4096, 8192], P(('dp', 'ctx', 'head')), parts along dimension 0
- attended: bfloat16 [4096, 4096], P(('dp', 'ctx'), 'head'), parts along dimension 0
There are 2 independent parts, one for each index of `dp`. A program takes and returns all parts, laid end to end along the dimension named above; an argument that names none is the same for every part. Nothing has to cross between parts.
Inputs may be any that keep to these rules, and one draw needn't show every extreme that they name: `doc_ids`: document numbers never fall along the sequence; every number occurs; each document covers 1 to 1536 tokens and one covers exactly 1536.
All inputs are finite; a program needn't handle non-finite values.
Results may differ from a plain program's by a relative error of at most 0.0049.
Values may be sent and summed in bfloat16 or wider, within the bound.
A program may use at most 128 MiB of HBM per device.

v0:
```python
import functools
import math

import jax
import jax.numpy as jnp
from jax import lax
from jax.experimental import pallas as pl
from jax.experimental.pallas import tpu as pltpu
from jax.sharding import PartitionSpec as P

HEAD_DIM = 128
DOCS = 4
NEG_FILL = -1e30
SCALE2 = math.log2(math.e) / math.sqrt(HEAD_DIM)
MIX_CHUNKS = 2
HEAD_CHUNKS = 2
STEP = 32
VMEM_BYTES = 48 * 1024 * 1024


def conv_kernel(groups, filt_ref, mask_ref, prev_ref, cur_ref, gate_ref, *rest):
    out_ref = rest[-1]
    taps = filt_ref.shape[1]
    lanes = prev_ref.shape[1]
    size = lanes // groups
    few = 16
    mask = mask_ref[...]
    filters = filt_ref[...].astype(jnp.float32)
    rows = jnp.concatenate([prev_ref[...].T, cur_ref[...].T], axis=1)

    def weight(g):
        row = jnp.broadcast_to(filters[g : g + 1], (few, taps))
        base = pltpu.roll(row, 0, 1, stride=1, stride_axis=0).astype(jnp.bfloat16)
        turns = [base] + [pltpu.roll(base, i, 1) for i in range(few, taps, few)]
        return jnp.concatenate(turns + turns, axis=0) * mask

    pieces = []
    for g in range(0, groups, 2):
        pair = jnp.concatenate([weight(g), weight(g + 1)], axis=1)
        both = jnp.dot(
            rows[g * size : (g + 2) * size], pair, preferred_element_type=jnp.float32
        )
        pieces += [both[:size, :taps], both[size:, taps:]]
    convolved = jnp.concatenate(pieces, axis=0).T
    out_ref[...] = (gate_ref[...].astype(jnp.float32) * convolved).astype(out_ref.dtype)


def convolve(chunk, filters, mask, prev, cur, gate, so_far):
    rows, width = prev.shape
    total = gate.shape[1]
    group_size = total // filters.shape[0]
    lanes = 512
    groups = lanes // group_size
    steps = width // lanes
    first = chunk * steps
    in_specs = [
        pl.BlockSpec((groups, filters.shape[1]), lambda i: (first + i, 0)),
        pl.BlockSpec(mask.shape, lambda i: (0, 0)),
        pl.BlockSpec((rows, lanes), lambda i: (0, i)),
        pl.BlockSpec((rows, lanes), lambda i: (0, i)),
        pl.BlockSpec((rows, lanes), lambda i: (0, first + i)),
    ]
    operands = [filters, mask, prev, cur, gate]
    aliases = {}
    if so_far is not None:
        in_specs.append(pl.BlockSpec(memory_space=pl.ANY))
        operands.append(so_far)
        aliases = {5: 0}
    return pl.pallas_call(
        functools.partial(conv_kernel, groups),
        grid=(steps,),
        out_shape=jax.ShapeDtypeStruct(gate.shape, gate.dtype),
        in_specs=in_specs,
        out_specs=pl.BlockSpec((rows, lanes), lambda i: (0, first + i)),
        input_output_aliases=aliases,
        compiler_params=pltpu.CompilerParams(vmem_limit_bytes=VMEM_BYTES),
        cost_estimate=pl.CostEstimate(
            flops=2 * rows * 2 * rows * 256 * width // group_size,
            bytes_accessed=4 * rows * width * 2,
            transcendentals=0,
        ),
    )(*operands)


def three_terms(x):
    high = x.astype(jnp.bfloat16).astype(jnp.float32)
    middle = (x - high).astype(jnp.bfloat16).astype(jnp.float32)
    return high, middle, x - high - middle


def attend_tiles(head, causal, use_far, q_ref, k_own, v_own, k_far, v_far, *refs):
    bias = refs[-1]
    out_ref = refs[-2]
    terms = out_ref.dtype == jnp.bfloat16
    stats = slice(out_ref.shape[1] - HEAD_DIM, out_ref.shape[1])
    place = pl.ds(pl.multiple_of(head * HEAD_DIM, HEAD_DIM), HEAD_DIM)
    own = k_own.shape[0]
    tile = 128
    count = q_ref.shape[0] // tile
    ones = jnp.ones((own, HEAD_DIM), jnp.bfloat16)
    wide_own = jnp.concatenate([v_own[...], ones], axis=1)
    wide_far = jnp.concatenate([v_far[...], ones], axis=1)
    lane = lax.broadcasted_iota(jnp.int32, (tile, HEAD_DIM), 1)

    def scores_of(i):
        here = slice(i * tile, (i + 1) * tile)
        seen = (i + 1) * tile if causal else own
        query = q_ref[here]
        dims = (((1,), (1,)), ((), ()))
        near = lax.dot_general(
            query, k_own[:seen], dims, preferred_element_type=jnp.float32
        )
        out = [near + bias[here, :seen]]
        if use_far:
            away = lax.dot_general(query, k_far[...], dims, preferred_element_type=jnp.float32)
            out.append(away + bias[here, own:])
        return out

    def finish(i, scores):
        here = slice(i * tile, (i + 1) * tile)
        top = jnp.max(scores[0], axis=1, keepdims=True)
        if use_far:
            top = jnp.maximum(top, jnp.max(scores[1], axis=1, keepdims=True))
        weights = [jnp.exp2((s - top) * SCALE2).astype(jnp.bfloat16) for s in scores]
        both = jnp.dot(
            weights[0], wide_own[: scores[0].shape[1]], preferred_element_type=jnp.float32
        )
        if use_far:
            both += jnp.dot(weights[1], wide_far, preferred_element_type=jnp.float32)
        total = both[:, HEAD_DIM:]
        out_ref[here, place] = (both[:, :HEAD_DIM] / total).astype(out_ref.dtype)
        lse = top * SCALE2 + jnp.log2(total)
        spread = out_ref[here, stats].astype(jnp.float32)
        if terms:
            for at, term in enumerate(three_terms(lse)):
                spread = jnp.where(lane == head + at * STEP, term, spread)
        else:
            spread = jnp.where(lane == head, lse, spread)
        out_ref[here, stats] = spread.astype(out_ref.dtype)

    ready = scores_of(0)
    for i in range(count):
        later = scores_of(i + 1) if i + 1 < count else None
        finish(i, ready)
        ready = later


def attend_kernel(causal, how_ref, low_ref, high_ref, kpos_ref, *refs):
    how = how_ref[0]
    head = pl.program_id(0)
    bias = refs[-1]

    @pl.when(head == 0)
    def _():
        out_ref = refs[-2]
        out_ref[...] = jnp.zeros_like(out_ref)

    @pl.when((head == 0) & (how > 0))
    def _():
        kpos = kpos_ref[...]
        allowed = (kpos >= low_ref[...]) & (kpos <= high_ref[...])
        bias[...] = jnp.where(allowed, 0.0, NEG_FILL)

    if causal:

        @pl.when(how == 1)
        def _():
            attend_tiles(head, causal, False, *refs)

    @pl.when(how == 2)
    def _():
        attend_tiles(head, causal, True, *refs)


def attend(how, low, high, kpos, query, own, far, first, heads, causal, out_type, after):
    rows = query.shape[0]
    width = (heads + 1) * HEAD_DIM
    keys = own[0].shape[0]
    block = pl.BlockSpec((rows, HEAD_DIM), lambda h: (0, first + h))
    whole = lambda shape: pl.BlockSpec(shape, lambda h: (0, 0))
    return pl.pallas_call(
        functools.partial(attend_kernel, causal),
        grid=(heads,),
        out_shape=jax.ShapeDtypeStruct((rows, width), out_type),
        in_specs=[
            pl.BlockSpec(memory_space=pltpu.SMEM),
            whole(low.shape),
            whole(high.shape),
            whole(kpos.shape),
        ]
        + [block] * 5
        + [pl.BlockSpec(memory_space=pl.ANY)] * len(after),
        out_specs=whole((rows, width)),
        scratch_shapes=[pltpu.VMEM((rows, 2 * keys), jnp.float32)],
        compiler_params=pltpu.CompilerParams(vmem_limit_bytes=VMEM_BYTES),
        cost_estimate=pl.CostEstimate(
            flops=12 * rows * 2 * keys * width,
            bytes_accessed=8 * rows * width,
            transcendentals=heads * rows * 2 * keys,
        ),
    )(how, low, high, kpos, query, *own, *far, *after)


def merge_kernel(heads, chunks, has_ref, o1_ref, *refs):
    out_ref = refs[-1]
    width = heads * HEAD_DIM
    has = has_ref[0]
    each = heads // chunks

    @pl.when(has == 0)
    def _():
        out_ref[...] = o1_ref[:, :width].astype(out_ref.dtype)

    @pl.when(has != 0)
    def _():
        first = o1_ref[:, width:]
        for c in range(chunks):
            o2_ref = refs[c]
            mine = first if c == 0 else pltpu.roll(first, HEAD_DIM - c * each, 1)
            sent = o2_ref[:, each * HEAD_DIM :].astype(jnp.float32)
            second = (
                sent
                + pltpu.roll(sent, HEAD_DIM - STEP, 1)
                + pltpu.roll(sent, HEAD_DIM - 2 * STEP, 1)
            )
            top = jnp.maximum(mine, second)
            one, two = jnp.exp2(mine - top), jnp.exp2(second - top)
            share = two / (one + two)
            for h in range(each):
                near = slice((c * each + h) * HEAD_DIM, (c * each + h + 1) * HEAD_DIM)
                cols = slice(h * HEAD_DIM, (h + 1) * HEAD_DIM)
                base = o1_ref[:, near]
                out_ref[:, near] = (
                    base + (o2_ref[:, cols].astype(jnp.float32) - base) * share[:, h : h + 1]
                ).astype(out_ref.dtype)


def merge(has, local, partials):
    rows = local.shape[0]
    width = local.shape[1] - HEAD_DIM
    heads = width // HEAD_DIM
    vmem = pl.BlockSpec(memory_space=pltpu.VMEM)
    return pl.pallas_call(
        functools.partial(merge_kernel, heads, len(partials)),
        out_shape=jax.ShapeDtypeStruct((rows, width), jnp.bfloat16),
        in_specs=[pl.BlockSpec(memory_space=pltpu.SMEM)] + [vmem] * (1 + len(partials)),
        out_specs=vmem,
        compiler_params=pltpu.CompilerParams(vmem_limit_bytes=VMEM_BYTES),
        cost_estimate=pl.CostEstimate(
            flops=4 * rows * width, bytes_accessed=8 * rows * width, transcendentals=0
        ),
    )(has, local, *partials)


def on_device(mix_query, mix_key, mix_value, mr_filter, doc_ids, att_query, att_key, att_value):
    ctx = lax.axis_index("ctx")
    ctx_size = lax.axis_size("ctx")
    half = ctx_size // 2
    assert ctx_size == 4
    swap = [(i, i ^ 1) for i in range(ctx_size)]
    back = [(i + half, i) for i in range(half)]
    forth = [(i, i + half) for i in range(half)]

    rows, width = att_query.shape
    far_query = lax.ppermute(att_query, "ctx", back)
    far = (lax.ppermute(att_key, "ctx", swap), lax.ppermute(att_value, "ctx", swap))
    own = (att_key, att_value)

    tok_rows, channels = mix_query.shape
    chunk = channels // MIX_CHUNKS
    peers = ctx_size * lax.axis_size("head")
    onward = [(i, i + 1) for i in range(peers - 1)]
    products, rims = [], []
    for c in range(MIX_CHUNKS):
        cols = slice(c * chunk, (c + 1) * chunk)
        product = (
            mix_key[:, cols].astype(jnp.float32) * mix_value[:, cols].astype(jnp.float32)
        ).astype(jnp.bfloat16)
        products.append(product)
        rims.append(lax.ppermute(product, ("ctx", "head"), onward))

    def of_block(block):
        begin = block * rows
        ids = lax.dynamic_slice_in_dim(doc_ids, begin, rows)
        low = jnp.zeros((rows,), jnp.int32)
        for doc in range(1, DOCS):
            before = jnp.sum((doc_ids < doc).astype(jnp.int32), dtype=jnp.int32)
            low = jnp.where(ids >= doc, before, low)
        return low[:, None], (begin + jnp.arange(rows, dtype=jnp.int32))[:, None]

    offset = jnp.arange(rows, dtype=jnp.int32)
    kpos = jnp.concatenate([ctx * rows + offset, (ctx ^ 1) * rows + offset])[None]
    local_how = jnp.where(ctx % 2 == 1, 2, 1).astype(jnp.int32)[None]
    far_how = jnp.where(ctx < half, 2, 0).astype(jnp.int32)[None]
    has = (ctx >= half).astype(jnp.int32)[None]
    local_rows = of_block(ctx)
    far_rows = of_block(jnp.minimum(ctx + half, ctx_size - 1))
    heads = width // HEAD_DIM
    each = heads // HEAD_CHUNKS
    local = attend(
        local_how, *local_rows, kpos, att_query, own, far, 0, heads, True, jnp.float32, ()
    )
    partials, after = [], (local,)
    for c in range(HEAD_CHUNKS):
        out = attend(
            far_how,
            *far_rows,
            kpos,
            far_query,
            own,
            far,
            c * each,
            each,
            False,
            jnp.bfloat16,
            after,
        )
        after = (out,)
        partials.append(lax.ppermute(out, "ctx", forth))
    attended = merge(has, local, partials)

    taps = mr_filter.shape[1]
    place = (ctx * lax.axis_size("head") + lax.axis_index("head")) * tok_rows
    padded_ids = jnp.concatenate([jnp.full((taps,), -1, jnp.int32), doc_ids])
    near_ids = lax.dynamic_slice_in_dim(padded_ids, place, tok_rows + taps)
    lag = jnp.arange(tok_rows)[None, :] + taps - jnp.arange(tok_rows + taps)[:, None]
    mask = (
        (lag >= 0) & (lag < taps) & (near_ids[:, None] == near_ids[None, taps:])
    ).astype(jnp.bfloat16)
    mixed = None
    for c in range(MIX_CHUNKS):
        mixed = convolve(c, mr_filter, mask, rims[c], products[c], mix_query, mixed)
    return (mixed, attended)


def solution(mesh):
    placed = (
        P(("dp", "ctx", "head"), None),
        P(("dp", "ctx", "head"), None),
        P(("dp", "ctx", "head"), None),
        P(),
        P("dp"),
        P(("dp", "ctx"), "head"),
        P(("dp", "ctx"), "head"),
        P(("dp", "ctx"), "head"),
    )
    return jax.shard_map(
        on_device,
        mesh=mesh,
        in_specs=placed,
        out_specs=(P(("dp", "ctx", "head"), None), P(("dp", "ctx"), "head")),
        check_vma=False,
    )
```

profile of v0, /device:TPU:7, one launch (start us, length us, event | category | flops | bytes accessed | tf_op | source)
XLA Modules:
  0.0 80.4 jit_solution(8426458161816605972)
XLA Ops:
  0.6 0.7 collective-permute-start.2
  1.5 3.1 %collective-permute-start.4 = (bf16[512,1024]{1,0:T(8,128)(2,1)}, bf16[512,1024]{1,0:T(8,128)(2,1)}, u32[]{:S(2)}, u32[]{:S(2)}) collective-permute-start(bf16[512,1024]{1,0:T(8,128)(2,1)} %refs_0_.1), channel_id=1, source_target_pairs={{8,0},{12,4},{9,1},{13,5},{10,2},{14,6},{11,3},{15,7},{24,16},{28,... | collective-permute-start | bytes 3145736 | tf_op jit(solution)/shard_map/ppermute | solution.py:265
  4.6 3.0 %multiply_convert_fusion = (bf16[128,4096]{1,0:T(8,128)(2,1)S(1)}, bf16[128,4096]{1,0:T(8,128)(2,1)S(1)}) fusion(bf16[128,8192]{1,0:T(8,128)(2,1)} %param.10, bf16[128,8192]{1,0:T(8,128)(2,1)} %param.9), kind=kLoop, calls=%fused_computation | loop fusion | flops 4194304 | bytes 6291456 | tf_op jit(solution)/shard_map/convert_element_type | solution.py:278
  7.5 3.2 %collective-permute-start.1 = (bf16[128,4096]{1,0:T(8,128)(2,1)S(1)}, bf16[128,4096]{1,0:T(8,128)(2,1)}, u32[]{:S(2)}, u32[]{:S(2)}) collective-permute-start(bf16[128,4096]{1,0:T(8,128)(2,1)S(1)} %get-tuple-element.5.cur_ref), channel_id=1, source_target_pairs={{0,1},{1,2},{2,3},{3,4},{4,5},{5,6},{6,7},{7,8},{8,9},{9,10},{10,1... | collective-permute-start | bytes 3145736 | tf_op jit(solution)/shard_map/ppermute | solution.py:280
  10.8 3.2 %collective-permute-start = (bf16[128,4096]{1,0:T(8,128)(2,1)S(1)}, bf16[128,4096]{1,0:T(8,128)(2,1)}, u32[]{:S(2)}, u32[]{:S(2)}) collective-permute-start(bf16[128,4096]{1,0:T(8,128)(2,1)S(1)} %get-tuple-element.6.cur_ref), channel_id=1, source_target_pairs={{0,1},{1,2},{2,3},{3,4},{4,5},{5,6},{6,7},{7,8},{8,9},{9,10},{10,1... | collective-permute-start | bytes 3145736 | tf_op jit(solution)/shard_map/ppermute | solution.py:280
  14.0 0.1 pad_dynamic-slice_fusion
  14.1 0.7 convert_reduce_fusion.2
  14.8 2.0 %select_select_fusion = (s32[512]{0:T(512)S(1)}, s32[512]{0:T(512)S(1)}) fusion(s32[2048]{0:T(1024)S(1)} %copy-done.8, s32[]{:T(128)S(6)} %select_n.50, s32[]{:T(128)} %get-tuple-element.4, s32[]{:T(128)} %get-tuple-element.3, s32[]{:T(128)} %get-tuple-element.2, s32[]{:T(128)S(6)} %select_n.45), kind=kLoop, calls=%fused_computation.15 | loop fusion | flops 6144 | bytes 8212 | tf_op jit(solution)/shard_map/jit(_where)/select_n | solution.py:288
  16.9 0.1 copy.11.low_ref
  17.0 0.1 copy.12.low_ref
  17.2 0.1 fusion.4.mask_ref
  17.4 1.2 %copy-done.2 = bf16[512,1024]{1,0:T(8,128)(2,1)S(1)} copy-done((bf16[512,1024]{1,0:T(8,128)(2,1)S(1)}, bf16[512,1024]{1,0:T(8,128)(2,1)}, u32[]{:S(2)}) %copy-start.2) | copy-done | bytes 1048600
  18.6 1.2 %copy-done.3 = bf16[512,1024]{1,0:T(8,128)(2,1)S(1)} copy-done((bf16[512,1024]{1,0:T(8,128)(2,1)S(1)}, bf16[512,1024]{1,0:T(8,128)(2,1)}, u32[]{:S(2)}) %copy-start.3) | copy-done | bytes 1048600
  19.8 1.2 %copy-done.5 = bf16[512,1024]{1,0:T(8,128)(2,1)S(1)} copy-done((bf16[512,1024]{1,0:T(8,128)(2,1)S(1)}, bf16[512,1024]{1,0:T(8,128)(2,1)}, u32[]{:S(2)}) %copy-start.5) | copy-done | bytes 1048600
  21.0 12.0 %shard_map.97.refs_5_.o1_ref = f32[512,1152]{1,0:T(8,128)} custom-call(s32[1]{0:T(128)} %bitcast.1.how_ref, s32[512,1]{1,0:T(8,128)S(1)} %copy.11.low_ref, s32[512,1]{1,0:T(8,128)S(1)} %iota_add_fusion.1.high_ref, s32[1,1024]{1,0:T(1,128)S(1)} %bitcast.6, bf16[512,1024]{1,0:T(8,128)(2,1)S(1)} %copy-done.2, bf16[512,1024]{1,0:T(8,128)(2,1)S(1)} %copy-done.3, ...), custom_call_target="tpu_custom_call" | custom-call | flops 7247757312 | bytes 4718592 | tf_op jit(solution)/shard_map/pallas_call | solution.py:181
  33.1 2.4 %shard_map.98.refs_5_ = bf16[512,640]{1,0:T(8,128)(2,1)S(1)} custom-call(s32[1]{0:T(128)} %bitcast.4.how_ref, s32[512,1]{1,0:T(8,128)S(1)} %copy.12.low_ref, s32[512,1]{1,0:T(8,128)S(1)} %iota_add_fusion.high_ref, s32[1,1024]{1,0:T(1,128)S(1)} %bitcast.7, bf16[512,1024]{1,0:T(8,128)(2,1)} %collective-permute-done.4.refs_0_, bf16[512,1024]{1,0:T(8,128)(2,1)S(1)} %copy-done.4, ...), custom_call_target="tpu_custom_call" | custom-call | flops 4026531840 | bytes 2621440 | tf_op jit(solution)/shard_map/pallas_call | solution.py:181
  35.5 1.4 %collective-permute-start.5 = (bf16[512,640]{1,0:T(8,128)(2,1)S(1)}, bf16[512,640]{1,0:T(8,128)(2,1)S(1)}, u32[]{:S(2)}, u32[]{:S(2)}) collective-permute-start(bf16[512,640]{1,0:T(8,128)(2,1)S(1)} %shard_map.98.refs_5_), channel_id=1, source_target_pairs={{0,8},{4,12},{1,9},{5,13},{2,10},{6,14},{3,11},{7,15},{16,24},{20,... | collective-permute-start | bytes 1966088 | tf_op jit(solution)/shard_map/ppermute | solution.py:319
  36.9 2.4 %shard_map.99 = bf16[512,640]{1,0:T(8,128)(2,1)S(1)} custom-call(s32[1]{0:T(128)} %bitcast.4.how_ref, s32[512,1]{1,0:T(8,128)S(1)} %copy.12.low_ref, s32[512,1]{1,0:T(8,128)S(1)} %iota_add_fusion.high_ref, s32[1,1024]{1,0:T(1,128)S(1)} %bitcast.8, bf16[512,1024]{1,0:T(8,128)(2,1)} %collective-permute-done.4.refs_0_, bf16[512,1024]{1,0:T(8,128)(2,1)S(1)} %copy-done.4, ...), custom_call_target="tpu_custom_call" | custom-call | flops 4026531840 | bytes 2621440 | tf_op jit(solution)/shard_map/pallas_call | solution.py:181
  39.3 1.3 %collective-permute-start.6 = (bf16[512,640]{1,0:T(8,128)(2,1)S(1)}, bf16[512,640]{1,0:T(8,128)(2,1)S(1)}, u32[]{:S(2)}, u32[]{:S(2)}) collective-permute-start(bf16[512,640]{1,0:T(8,128)(2,1)S(1)} %shard_map.99), channel_id=1, source_target_pairs={{0,8},{4,12},{1,9},{5,13},{2,10},{6,14},{3,11},{7,15},{16,24},{20,... | collective-permute-start | bytes 1966088 | tf_op jit(solution)/shard_map/ppermute | solution.py:319
  40.6 8.8 %shard_map.95.rest_0_ = bf16[128,8192]{1,0:T(8,128)(2,1)} custom-call(bf16[512,128]{1,0:T(8,128)(2,1)S(1)} %copy-done.7, bf16[256,128]{1,0:T(8,128)(2,1)S(1)} %fusion.4.mask_ref, bf16[128,4096]{1,0:T(8,128)(2,1)} %collective-permute-done.1.prev_ref, bf16[128,4096]{1,0:T(8,128)(2,1)S(1)} %get-tuple-element.5.cur_ref, bf16[128,8192]{1,0:T(8,128)(2,1)S(1)} %copy-done.1), custom_call_target="tpu_custom_call" | custom-call | flops 4294967296 | bytes 4194304 | tf_op jit(solution)/shard_map/pallas_call | solution.py:69
  49.5 5.5 %collective-permute-done.prev_ref = bf16[128,4096]{1,0:T(8,128)(2,1)} collective-permute-done((bf16[128,4096]{1,0:T(8,128)(2,1)S(1)}, bf16[128,4096]{1,0:T(8,128)(2,1)}, u32[]{:S(2)}, u32[]{:S(2)}) %collective-permute-start) | collective-permute-done | bytes 1048608 | tf_op jit(solution)/shard_map/ppermute | solution.py:280
  55.0 8.9 %shard_map.96 = bf16[128,8192]{1,0:T(8,128)(2,1)} custom-call(bf16[512,128]{1,0:T(8,128)(2,1)S(1)} %copy-done.7, bf16[256,128]{1,0:T(8,128)(2,1)S(1)} %fusion.4.mask_ref, bf16[128,4096]{1,0:T(8,128)(2,1)} %collective-permute-done.prev_ref, bf16[128,4096]{1,0:T(8,128)(2,1)S(1)} %get-tuple-element.6.cur_ref, ...), custom_call_target="tpu_custom_call", output_to_operand_aliasing={{}: (5, {})} | custom-call | flops 4294967296 | bytes 4194304 | tf_op jit(solution)/shard_map/pallas_call | solution.py:69
  63.9 14.4 %collective-permute-done.6.refs_1_ = bf16[512,640]{1,0:T(8,128)(2,1)S(1)} collective-permute-done((bf16[512,640]{1,0:T(8,128)(2,1)S(1)}, bf16[512,640]{1,0:T(8,128)(2,1)S(1)}, u32[]{:S(2)}, u32[]{:S(2)}) %collective-permute-start.6) | collective-permute-done | bytes 655392 | tf_op jit(solution)/shard_map/ppermute | solution.py:319
  78.3 2.1 %shard_map.100 = bf16[512,1024]{1,0:T(8,128)(2,1)} custom-call(s32[1]{0:T(128)} %bitcast.has_ref, f32[512,1152]{1,0:T(8,128)S(1)} %copy-done, bf16[512,640]{1,0:T(8,128)(2,1)S(1)} %collective-permute-done.5.refs_0_, bf16[512,640]{1,0:T(8,128)(2,1)S(1)} %collective-permute-done.6.refs_1_), custom_call_target="tpu_custom_call" | custom-call | flops 2097152 | bytes 4194304 | tf_op jit(solution)/shard_map/pallas_call | solution.py:243
  (27 shorter events, 0.2 us)
Async XLA Ops:
  0.6 13.4 %copy-start.8 = (s32[2048]{0:T(1024)S(1)}, s32[2048]{0:T(1024)}, u32[]{:S(2)}) copy-start(s32[2048]{0:T(1024)} %param.12) | copy-start | bytes 24580
  0.6 16.7 %collective-permute-start.2 = (bf16[512,1024]{1,0:T(8,128)(2,1)}, bf16[512,1024]{1,0:T(8,128)(2,1)}, u32[]{:S(2)}, u32[]{:S(2)}) collective-permute-start(bf16[512,1024]{1,0:T(8,128)(2,1)} %refs_1_.5), channel_id=1, source_target_pairs={{0,4},{4,0},{8,12},{12,8},{1,5},{5,1},{9,13},{13,9},{2,6},{6,2},{1... | collective-permute-start | bytes 3145736 | tf_op jit(solution)/shard_map/ppermute | solution.py:266
  1.4 16.0 %collective-permute-start.3 = (bf16[512,1024]{1,0:T(8,128)(2,1)}, bf16[512,1024]{1,0:T(8,128)(2,1)}, u32[]{:S(2)}, u32[]{:S(2)}) collective-permute-start(bf16[512,1024]{1,0:T(8,128)(2,1)} %refs_2_.5), channel_id=1, source_target_pairs={{0,4},{4,0},{8,12},{12,8},{1,5},{5,1},{9,13},{13,9},{2,6},{6,2},{1... | collective-permute-start | bytes 3145736 | tf_op jit(solution)/shard_map/ppermute | solution.py:266
  1.5 31.6 %collective-permute-start.4 = (bf16[512,1024]{1,0:T(8,128)(2,1)}, bf16[512,1024]{1,0:T(8,128)(2,1)}, u32[]{:S(2)}, u32[]{:S(2)}) collective-permute-start(bf16[512,1024]{1,0:T(8,128)(2,1)} %refs_0_.1), channel_id=1, source_target_pairs={{8,0},{12,4},{9,1},{13,5},{10,2},{14,6},{11,3},{15,7},{24,16},{28,... | collective-permute-start | bytes 3145736 | tf_op jit(solution)/shard_map/ppermute | solution.py:265
  7.5 33.1 %collective-permute-start.1 = (bf16[128,4096]{1,0:T(8,128)(2,1)S(1)}, bf16[128,4096]{1,0:T(8,128)(2,1)}, u32[]{:S(2)}, u32[]{:S(2)}) collective-permute-start(bf16[128,4096]{1,0:T(8,128)(2,1)S(1)} %get-tuple-element.5.cur_ref), channel_id=1, source_target_pairs={{0,1},{1,2},{2,3},{3,4},{4,5},{5,6},{6,7},{7,8},{8,9},{9,10},{10,1... | collective-permute-start | bytes 3145736 | tf_op jit(solution)/shard_map/ppermute | solution.py:280
  10.8 44.2 %collective-permute-start = (bf16[128,4096]{1,0:T(8,128)(2,1)S(1)}, bf16[128,4096]{1,0:T(8,128)(2,1)}, u32[]{:S(2)}, u32[]{:S(2)}) collective-permute-start(bf16[128,4096]{1,0:T(8,128)(2,1)S(1)} %get-tuple-element.6.cur_ref), channel_id=1, source_target_pairs={{0,1},{1,2},{2,3},{3,4},{4,5},{5,6},{6,7},{7,8},{8,9},{9,10},{10,1... | collective-permute-start | bytes 3145736 | tf_op jit(solution)/shard_map/ppermute | solution.py:280
  17.4 1.2 %copy-start.2 = (bf16[512,1024]{1,0:T(8,128)(2,1)S(1)}, bf16[512,1024]{1,0:T(8,128)(2,1)}, u32[]{:S(2)}) copy-start(bf16[512,1024]{1,0:T(8,128)(2,1)} %refs_0_.1) | copy-start | bytes 3145732
  18.6 1.2 %copy-start.3 = (bf16[512,1024]{1,0:T(8,128)(2,1)S(1)}, bf16[512,1024]{1,0:T(8,128)(2,1)}, u32[]{:S(2)}) copy-start(bf16[512,1024]{1,0:T(8,128)(2,1)} %refs_1_.5) | copy-start | bytes 3145732
  19.8 1.2 %copy-start.5 = (bf16[512,1024]{1,0:T(8,128)(2,1)S(1)}, bf16[512,1024]{1,0:T(8,128)(2,1)}, u32[]{:S(2)}) copy-start(bf16[512,1024]{1,0:T(8,128)(2,1)} %refs_2_.5) | copy-start | bytes 3145732
  21.0 12.1 %copy-start.4 = (bf16[512,1024]{1,0:T(8,128)(2,1)S(1)}, bf16[512,1024]{1,0:T(8,128)(2,1)}, u32[]{:S(2)}) copy-start(bf16[512,1024]{1,0:T(8,128)(2,1)} %refs_1_.5) | copy-start | bytes 3145732
  21.0 12.1 %copy-start.6 = (bf16[512,1024]{1,0:T(8,128)(2,1)S(1)}, bf16[512,1024]{1,0:T(8,128)(2,1)}, u32[]{:S(2)}) copy-start(bf16[512,1024]{1,0:T(8,128)(2,1)} %refs_2_.5) | copy-start | bytes 3145732
  35.5 5.1 %copy-start.1 = (bf16[128,8192]{1,0:T(8,128)(2,1)S(1)}, bf16[128,8192]{1,0:T(8,128)(2,1)}, u32[]{:S(2)}) copy-start(bf16[128,8192]{1,0:T(8,128)(2,1)} %gate_ref.3) | copy-start | bytes 6291460
  35.5 5.1 %copy-start.7 = (bf16[512,128]{1,0:T(8,128)(2,1)S(1)}, bf16[512,128]{1,0:T(8,128)(2,1)}, u32[]{:S(2)}) copy-start(bf16[512,128]{1,0:T(8,128)(2,1)} %filt_ref.3) | copy-start | bytes 393220
  35.5 42.8 %collective-permute-start.5 = (bf16[512,640]{1,0:T(8,128)(2,1)S(1)}, bf16[512,640]{1,0:T(8,128)(2,1)S(1)}, u32[]{:S(2)}, u32[]{:S(2)}) collective-permute-start(bf16[512,640]{1,0:T(8,128)(2,1)S(1)} %shard_map.98.refs_5_), channel_id=1, source_target_pairs={{0,8},{4,12},{1,9},{5,13},{2,10},{6,14},{3,11},{7,15},{16,24},{20,... | collective-permute-start | bytes 1966088 | tf_op jit(solution)/shard_map/ppermute | solution.py:319
  39.3 39.0 %collective-permute-start.6 = (bf16[512,640]{1,0:T(8,128)(2,1)S(1)}, bf16[512,640]{1,0:T(8,128)(2,1)S(1)}, u32[]{:S(2)}, u32[]{:S(2)}) collective-permute-start(bf16[512,640]{1,0:T(8,128)(2,1)S(1)} %shard_map.99), channel_id=1, source_target_pairs={{0,8},{4,12},{1,9},{5,13},{2,10},{6,14},{3,11},{7,15},{16,24},{20,... | collective-permute-start | bytes 1966088 | tf_op jit(solution)/shard_map/ppermute | solution.py:319
  49.5 28.8 %copy-start = (f32[512,1152]{1,0:T(8,128)S(1)}, f32[512,1152]{1,0:T(8,128)}, u32[]{:S(2)}) copy-start(f32[512,1152]{1,0:T(8,128)} %shard_map.97.refs_5_.o1_ref) | copy-start | bytes 7077892
where the time goes:
time: 81.3 us; the launch traced here: 80.4 us
  Pallas kernels  36.7 us (45%)
  waiting for transfers between devices  20 us (25%)
  starting transfers between devices  13.1 us (16%)
  other arithmetic  5.84 us (7%)
  local copies, waits for them, and re-layouts  4.07 us (5%)
  between operations  0.83 us (1%)
    pallas_call x2, Pallas kernels, convolve(): pl.pallas_call(functools.partial(conv_kernel, groups), grid=(steps,), out...  17.7 us
    pallas_call x3, Pallas kernels, attend(): pl.pallas_call(functools.partial(attend_kernel, causal), grid=(heads,), o...  16.8 us
    ppermute x2, waiting for transfers between devices, on_device(): partials.append(lax.ppermute(out, 'ctx', forth))  14.4 us
    ppermute x2, starting transfers between devices, on_device(): rims.append(lax.ppermute(product, ('ctx', 'head'), onward))  6.41 us
    ppermute x2, waiting for transfers between devices, on_device(): rims.append(lax.ppermute(product, ('ctx', 'head'), onward))  5.52 us
    unnamed x18, local copies, waits for them, and re-layouts  3.69 us
    ppermute x1, starting transfers between devices, on_device(): far_query = lax.ppermute(att_query, 'ctx', back)  3.12 us
    convert_element_type x1, other arithmetic, on_device(): product = (mix_key[:, cols].astype(jnp.float32) * mix_value[:, cols].asty...  2.95 us
  transfers between devices with their start and end apart: 7, of which 2 were waited for; matrix products, arithmetic and copies ran while one was open for 8% of the time, Pallas kernels for 43%

commit v1 on v0

--- a/solution.py
+++ b/solution.py
@@ -13,9 +13,9 @@
 NEG_FILL = -1e30
 SCALE2 = math.log2(math.e) / math.sqrt(HEAD_DIM)
 MIX_CHUNKS = 2
-HEAD_CHUNKS = 2
 STEP = 32
-VMEM_BYTES = 48 * 1024 * 1024
+DECLARED = 1 << 20
+VMEM_BYTES = 60 * 1024 * 1024
 
 
 def conv_kernel(groups, filt_ref, mask_ref, prev_ref, cur_ref, gate_ref, *rest):
@@ -45,7 +45,7 @@
     out_ref[...] = (gate_ref[...].astype(jnp.float32) * convolved).astype(out_ref.dtype)
 
 
-def convolve(chunk, filters, mask, prev, cur, gate, so_far):
+def convolve(chunk, filters, mask, prev, cur, gate, so_far, after):
     rows, width = prev.shape
     total = gate.shape[1]
     group_size = total // filters.shape[0]
@@ -66,6 +66,9 @@
         in_specs.append(pl.BlockSpec(memory_space=pl.ANY))
         operands.append(so_far)
         aliases = {5: 0}
+    else:
+        in_specs.append(pl.BlockSpec(memory_space=pl.ANY))
+        operands.append(after)
     return pl.pallas_call(
         functools.partial(conv_kernel, groups),
         grid=(steps,),
@@ -75,9 +78,7 @@
         input_output_aliases=aliases,
         compiler_params=pltpu.CompilerParams(vmem_limit_bytes=VMEM_BYTES),
         cost_estimate=pl.CostEstimate(
-            flops=2 * rows * 2 * rows * 256 * width // group_size,
-            bytes_accessed=4 * rows * width * 2,
-            transcendentals=0,
+            flops=DECLARED, bytes_accessed=DECLARED, transcendentals=0
         ),
     )(*operands)
 
@@ -145,20 +146,27 @@
         ready = later
 
 
-def attend_kernel(causal, how_ref, low_ref, high_ref, kpos_ref, *refs):
-    how = how_ref[0]
+def attend_kernel(causal, info_ref, *refs):
+    how = info_ref[0]
     head = pl.program_id(0)
-    bias = refs[-1]
-
-    @pl.when(head == 0)
-    def _():
-        out_ref = refs[-2]
-        out_ref[...] = jnp.zeros_like(out_ref)
+    refs = refs[:5] + refs[-2:]
+    out_ref, bias = refs[-2:]
+    rows, keys = bias.shape
 
     @pl.when((head == 0) & (how > 0))
     def _():
-        kpos = kpos_ref[...]
-        allowed = (kpos >= low_ref[...]) & (kpos <= high_ref[...])
+        stats = slice(out_ref.shape[1] - HEAD_DIM, out_ref.shape[1])
+        out_ref[:, stats] = jnp.zeros((rows, HEAD_DIM), out_ref.dtype)
+        at = info_ref[1] + lax.broadcasted_iota(jnp.int32, (rows, 1), 0)
+        low = jnp.zeros_like(at)
+        for doc in range(DOCS - 1):
+            begin = info_ref[4 + doc]
+            low = jnp.where(at >= begin, begin, low)
+        lane = lax.broadcasted_iota(jnp.int32, (1, keys), 1)
+        kpos = jnp.where(
+            lane < keys // 2, info_ref[2] + lane, info_ref[3] + lane - keys // 2
+        )
+        allowed = (kpos >= low) & (kpos <= at)
         bias[...] = jnp.where(allowed, 0.0, NEG_FILL)
 
     if causal:
@@ -172,52 +180,51 @@
         attend_tiles(head, causal, True, *refs)
 
 
-def attend(how, low, high, kpos, query, own, far, first, heads, causal, out_type, after):
-    rows = query.shape[0]
+def attend(info, heads, causal, out_type, operands, after):
+    rows = operands[0][0].shape[0]
     width = (heads + 1) * HEAD_DIM
-    keys = own[0].shape[0]
-    block = pl.BlockSpec((rows, HEAD_DIM), lambda h: (0, first + h))
-    whole = lambda shape: pl.BlockSpec(shape, lambda h: (0, 0))
+    keys = operands[1][0].shape[0]
+
+    def block(first, size):
+        def at(h, info_ref):
+            return (0, first + jnp.where(info_ref[0] > 0, h, 0))
+
+        return pl.BlockSpec((size, HEAD_DIM), at)
+
     return pl.pallas_call(
         functools.partial(attend_kernel, causal),
-        grid=(heads,),
+        grid_spec=pltpu.PrefetchScalarGridSpec(
+            num_scalar_prefetch=1,
+            grid=(heads,),
+            in_specs=[block(first, x.shape[0]) for x, first in operands]
+            + [pl.BlockSpec(memory_space=pl.ANY)] * len(after),
+            out_specs=pl.BlockSpec((rows, width), lambda h, info_ref: (0, 0)),
+            scratch_shapes=[pltpu.VMEM((rows, 2 * keys), jnp.float32)],
+        ),
         out_shape=jax.ShapeDtypeStruct((rows, width), out_type),
-        in_specs=[
-            pl.BlockSpec(memory_space=pltpu.SMEM),
-            whole(low.shape),
-            whole(high.shape),
-            whole(kpos.shape),
-        ]
-        + [block] * 5
-        + [pl.BlockSpec(memory_space=pl.ANY)] * len(after),
-        out_specs=whole((rows, width)),
-        scratch_shapes=[pltpu.VMEM((rows, 2 * keys), jnp.float32)],
         compiler_params=pltpu.CompilerParams(vmem_limit_bytes=VMEM_BYTES),
         cost_estimate=pl.CostEstimate(
-            flops=12 * rows * 2 * keys * width,
-            bytes_accessed=8 * rows * width,
-            transcendentals=heads * rows * 2 * keys,
+            flops=DECLARED, bytes_accessed=DECLARED, transcendentals=0
         ),
-    )(how, low, high, kpos, query, *own, *far, *after)
-
-
-def merge_kernel(heads, chunks, has_ref, o1_ref, *refs):
+    )(info, *[x for x, _ in operands], *after)
+
+
+def merge_kernel(each, chunks, has_ref, *refs):
     out_ref = refs[-1]
-    width = heads * HEAD_DIM
     has = has_ref[0]
-    each = heads // chunks
+    width = each * HEAD_DIM
 
     @pl.when(has == 0)
     def _():
-        out_ref[...] = o1_ref[:, :width].astype(out_ref.dtype)
+        for c in range(chunks):
+            out_ref[:, c * width : (c + 1) * width] = refs[2 * c][:, :width].astype(out_ref.dtype)
 
     @pl.when(has != 0)
     def _():
-        first = o1_ref[:, width:]
         for c in range(chunks):
-            o2_ref = refs[c]
-            mine = first if c == 0 else pltpu.roll(first, HEAD_DIM - c * each, 1)
-            sent = o2_ref[:, each * HEAD_DIM :].astype(jnp.float32)
+            o1_ref, o2_ref = refs[2 * c : 2 * c + 2]
+            mine = o1_ref[:, width:]
+            sent = o2_ref[:, width:].astype(jnp.float32)
             second = (
                 sent
                 + pltpu.roll(sent, HEAD_DIM - STEP, 1)
@@ -227,29 +234,29 @@
             one, two = jnp.exp2(mine - top), jnp.exp2(second - top)
             share = two / (one + two)
             for h in range(each):
-                near = slice((c * each + h) * HEAD_DIM, (c * each + h + 1) * HEAD_DIM)
                 cols = slice(h * HEAD_DIM, (h + 1) * HEAD_DIM)
-                base = o1_ref[:, near]
-                out_ref[:, near] = (
-                    base + (o2_ref[:, cols].astype(jnp.float32) - base) * share[:, h : h + 1]
-                ).astype(out_ref.dtype)
-
-
-def merge(has, local, partials):
-    rows = local.shape[0]
-    width = local.shape[1] - HEAD_DIM
-    heads = width // HEAD_DIM
+                base = o1_ref[:, cols]
+                mixed = base + (o2_ref[:, cols].astype(jnp.float32) - base) * share[:, h : h + 1]
+                at = c * width + h * HEAD_DIM
+                out_ref[:, at : at + HEAD_DIM] = mixed.astype(out_ref.dtype)
+
+
+def merge(has, pairs, after):
+    rows, wide = pairs[0][0].shape
+    width = wide - HEAD_DIM
     vmem = pl.BlockSpec(memory_space=pltpu.VMEM)
+    flat = [x for pair in pairs for x in pair]
     return pl.pallas_call(
-        functools.partial(merge_kernel, heads, len(partials)),
-        out_shape=jax.ShapeDtypeStruct((rows, width), jnp.bfloat16),
-        in_specs=[pl.BlockSpec(memory_space=pltpu.SMEM)] + [vmem] * (1 + len(partials)),
+        functools.partial(merge_kernel, width // HEAD_DIM, len(pairs)),
+        out_shape=jax.ShapeDtypeStruct((rows, width * len(pairs)), jnp.bfloat16),
+        in_specs=[pl.BlockSpec(memory_space=pltpu.SMEM)] + [vmem] * len(flat)
+        + [pl.BlockSpec(memory_space=pl.ANY)],
         out_specs=vmem,
         compiler_params=pltpu.CompilerParams(vmem_limit_bytes=VMEM_BYTES),
         cost_estimate=pl.CostEstimate(
-            flops=4 * rows * width, bytes_accessed=8 * rows * width, transcendentals=0
+            flops=DECLARED, bytes_accessed=DECLARED, transcendentals=0
         ),
-    )(has, local, *partials)
+    )(has, *flat, after)
 
 
 def on_device(mix_query, mix_key, mix_value, mr_filter, doc_ids, att_query, att_key, att_value):
@@ -262,9 +269,13 @@
     forth = [(i, i + half) for i in range(half)]
 
     rows, width = att_query.shape
-    far_query = lax.ppermute(att_query, "ctx", back)
-    far = (lax.ppermute(att_key, "ctx", swap), lax.ppermute(att_value, "ctx", swap))
-    own = (att_key, att_value)
+    cut = width // 2
+    low_pack = jnp.concatenate([att_key[:, :cut], att_value[:, :cut]], axis=1)
+    high_pack = jnp.concatenate([att_key[:, cut:], att_value[:, cut:]], axis=1)
+    on_first = ctx < half
+    over = lax.ppermute(jnp.where(on_first, low_pack, att_query), "ctx", forth + back)
+    low_swap = lax.ppermute(low_pack, "ctx", swap)
+    high_swap = lax.ppermute(high_pack, "ctx", swap)
 
     tok_rows, channels = mix_query.shape
     chunk = channels // MIX_CHUNKS
@@ -278,46 +289,55 @@
         ).astype(jnp.bfloat16)
         products.append(product)
         rims.append(lax.ppermute(product, ("ctx", "head"), onward))
-
-    def of_block(block):
-        begin = block * rows
-        ids = lax.dynamic_slice_in_dim(doc_ids, begin, rows)
-        low = jnp.zeros((rows,), jnp.int32)
-        for doc in range(1, DOCS):
-            before = jnp.sum((doc_ids < doc).astype(jnp.int32), dtype=jnp.int32)
-            low = jnp.where(ids >= doc, before, low)
-        return low[:, None], (begin + jnp.arange(rows, dtype=jnp.int32))[:, None]
-
-    offset = jnp.arange(rows, dtype=jnp.int32)
-    kpos = jnp.concatenate([ctx * rows + offset, (ctx ^ 1) * rows + offset])[None]
-    local_how = jnp.where(ctx % 2 == 1, 2, 1).astype(jnp.int32)[None]
-    far_how = jnp.where(ctx < half, 2, 0).astype(jnp.int32)[None]
+    begins = [
+        jnp.sum((doc_ids < doc).astype(jnp.int32), dtype=jnp.int32) for doc in range(1, DOCS)
+    ]
+
+    def info(how, query_block, own_block, other_block):
+        blocks = [x * rows for x in (query_block, own_block, other_block)]
+        return jnp.stack([jnp.asarray(x, jnp.int32) for x in [how] + blocks + begins])
+
+    each = width // 2 // HEAD_DIM
+    local_info = info(jnp.where(ctx % 2 == 1, 2, 1), ctx, ctx, ctx ^ 1)
+    high_info = info(jnp.where(on_first, 2, 0), ctx + half, ctx, ctx ^ 1)
+    low_info = info(jnp.where(on_first, 0, 2), ctx, ctx - half, (ctx - half) ^ 1)
+
+    local_low = attend(
+        local_info,
+        each,
+        True,
+        jnp.float32,
+        [(att_query, 0), (att_key, 0), (att_value, 0), (low_swap, 0), (low_swap, each)],
+        (),
+    )
+    local_high = attend(
+        local_info,
+        each,
+        True,
+        jnp.float32,
+        [(att_query, each), (att_key, each), (att_value, each), (high_swap, 0), (high_swap, each)],
+        (local_low,),
+    )
+    over, local_high = lax.optimization_barrier((over, local_high))
+    cross = lax.ppermute(over, "ctx", swap[half:])
+    far_high = attend(
+        high_info,
+        each,
+        False,
+        jnp.bfloat16,
+        [(over, each), (att_key, each), (att_value, each), (high_swap, 0), (high_swap, each)],
+        (local_high,),
+    )
+    high_forth = lax.ppermute(far_high, "ctx", forth)
+    far_low = attend(
+        low_info,
+        each,
+        False,
+        jnp.bfloat16,
+        [(att_query, 0), (over, 0), (over, each), (cross, 0), (cross, each)],
+        (far_high, rims[0]),
+    )
     has = (ctx >= half).astype(jnp.int32)[None]
-    local_rows = of_block(ctx)
-    far_rows = of_block(jnp.minimum(ctx + half, ctx_size - 1))
-    heads = width // HEAD_DIM
-    each = heads // HEAD_CHUNKS
-    local = attend(
-        local_how, *local_rows, kpos, att_query, own, far, 0, heads, True, jnp.float32, ()
-    )
-    partials, after = [], (local,)
-    for c in range(HEAD_CHUNKS):
-        out = attend(
-            far_how,
-            *far_rows,
-            kpos,
-            far_query,
-            own,
-            far,
-            c * each,
-            each,
-            False,
-            jnp.bfloat16,
-            after,
-        )
-        after = (out,)
-        partials.append(lax.ppermute(out, "ctx", forth))
-    attended = merge(has, local, partials)
 
     taps = mr_filter.shape[1]
     place = (ctx * lax.axis_size("head") + lax.axis_index("head")) * tok_rows
@@ -329,7 +349,8 @@
     ).astype(jnp.bfloat16)
     mixed = None
     for c in range(MIX_CHUNKS):
-        mixed = convolve(c, mr_filter, mask, rims[c], products[c], mix_query, mixed)
+        mixed = convolve(c, mr_filter, mask, rims[c], products[c], mix_query, mixed, far_low)
+    attended = merge(has, [(local_low, far_low), (local_high, high_forth)], mixed)
     return (mixed, attended)
 
 

time: 81.3 us -> 90.3 us (1.11)
  Pallas kernels: 36.7 us -> 48.3 us
  waiting for transfers between devices: 20 us -> 11.3 us
  local copies, waits for them, and re-layouts: 4.07 us -> 11.7 us
  starting transfers between devices: 13.1 us -> 10.5 us
    pallas_call x4 -> x5, Pallas kernels: 19 us -> 29.3 us  [the longest x4 25.1 us: attend(): pl.pallas_call(functools.partial(attend_kernel, causal), grid_spec=pltpu....]
    another operation x0 -> x3, local copies, waits for them, and re-layouts: none -> 7.48 us  [info(): jnp.stack([jnp.asarray(x, jnp.int32) for x in [how] + blocks + begins])]
    ppermute x2, waiting for transfers between devices: 5.52 us -> 0.01 us  [on_device(): rims.append(lax.ppermute(product, ('ctx', 'head'), onward))]
    ppermute x5, waiting for transfers between devices: 14.4 us -> 11.3 us  [the longest x1 11.3 us: on_device(): lax.ppermute(jnp.where(on_first, low_pack, att_query), 'ctx', forth + back)]
    concatenate x1 -> x2, other arithmetic: 0.01 us -> 2.96 us  [the longest x1 1.84 us: on_device(): low_pack = jnp.concatenate([att_key[:, :cut], att_value[:, :cut]], axis=1)]
    select_n x1 -> x0, other arithmetic: 1.99 us -> none  [of_block(): low = jnp.where(ids >= doc, before, low)]
    slice x0 -> x1, local copies, waits for them, and re-layouts: none -> 1.66 us  [on_device(): high_pack = jnp.concatenate([att_key[:, cut:], att_value[:, cut:]], axis=1)]
    pallas_call x2, Pallas kernels: 17.7 us -> 19.1 us  [convolve(): pl.pallas_call(functools.partial(conv_kernel, groups), grid=(steps,), out...]
  transfers between devices with their start and end apart: 7 -> 7, of which waited for: 2 -> 1; matrix products, arithmetic and copies ran while one was open for 8% -> 14% of each run, Pallas kernels for 43% -> 50%
where the time goes in v1:
time: 90.3 us; the launch traced here: 88.8 us
  Pallas kernels  48.3 us (53%)
  local copies, waits for them, and re-layouts  11.7 us (13%)
  waiting for transfers between devices  11.3 us (13%)
  starting transfers between devices  10.5 us (12%)
  other arithmetic  6.2 us (7%)
    pallas_call x4, Pallas kernels, attend(): pl.pallas_call(functools.partial(attend_kernel, causal), grid_spec=pltpu....  25.1 us
    pallas_call x2, Pallas kernels, convolve(): pl.pallas_call(functools.partial(conv_kernel, groups), grid=(steps,), out...  19.1 us
    ppermute x1, waiting for transfers between devices, on_device(): lax.ppermute(jnp.where(on_first, low_pack, att_query), 'ctx', forth + back)  11.3 us
    another operation x3, local copies, waits for them, and re-layouts, info(): jnp.stack([jnp.asarray(x, jnp.int32) for x in [how] + blocks + begins])  7.48 us
    ppermute x2, starting transfers between devices, on_device(): rims.append(lax.ppermute(product, ('ctx', 'head'), onward))  5.12 us
    pallas_call x1, Pallas kernels, merge(): pl.pallas_call(functools.partial(merge_kernel, width // HEAD_DIM, len(pai...  4.14 us
    ppermute x1, starting transfers between devices, on_device(): cross = lax.ppermute(over, 'ctx', swap[half:])  2.76 us
    unnamed x16, local copies, waits for them, and re-layouts  2.44 us
  transfers between devices with their start and end apart: 7, of which 1 were waited for; matrix products, arithmetic and copies ran while one was open for 14% of the time, Pallas kernels for 50%

profile of v1, /device:TPU:7, one launch (start us, length us, event | category | flops | bytes accessed | tf_op | source)
XLA Modules:
  0.0 88.8 jit_solution(547019783866573948)
XLA Ops:
  0.6 1.7 %fusion.5 = (bf16[512,512]{1,0:T(8,128)(2,1)S(1)}, bf16[512,512]{1,0:T(8,128)(2,1)S(1)}, bf16[512,512]{1,0:T(8,128)(2,1)S(1)}, bf16[512,512]{1,0:T(8,128)(2,1)S(1)}) fusion(bf16[512,1024]{1,0:T(8,128)(2,1)} %refs_1_.5, bf16[512,1024]{1,0:T(8,128)(2,1)} %refs_2_.5), kind=kLoop, calls=%fused_computation.16 | loop fusion | bytes 4194304 | tf_op jit(solution)/shard_map/slice | solution.py:274
  2.3 1.1 %pad_maximum_fusion.1 = bf16[512,1024]{1,0:T(8,128)(2,1)} fusion(bf16[512,512]{1,0:T(8,128)(2,1)S(1)} %get-tuple-element.18, bf16[512,512]{1,0:T(8,128)(2,1)S(1)} %get-tuple-element.13), kind=kLoop, calls=%fused_computation.3 | loop fusion | flops 2097152 | bytes 2097152 | tf_op jit(solution)/shard_map/concatenate | solution.py:274
  3.4 0.7 collective-permute-start.3
  4.1 1.8 %pad_maximum_fusion = (bf16[512,1024]{1,0:T(8,128)(2,1)}, bf16[512,1024]{1,0:T(8,128)(2,1)}) fusion(bf16[512,512]{1,0:T(8,128)(2,1)S(1)} %get-tuple-element.17, bf16[512,512]{1,0:T(8,128)(2,1)S(1)} %get-tuple-element.14, bf16[512,1024]{1,0:T(8,128)(2,1)S(1)} %copy-done.1, pred[]{:T(512)S(6)} %lt.39), kind=kLoop, calls=%fused_computation.2 | loop fusion | flops 2621440 | bytes 4194305 | tf_op jit(solution)/shard_map/concatenate | solution.py:273
  7.1 1.8 %multiply_convert_fusion = (bf16[128,4096]{1,0:T(8,128)(2,1)S(1)}, bf16[128,4096]{1,0:T(8,128)(2,1)}) fusion(bf16[128,8192]{1,0:T(8,128)(2,1)S(1)} %copy-done.5, bf16[128,8192]{1,0:T(8,128)(2,1)S(1)} %copy-done.6), kind=kLoop, calls=%fused_computation | loop fusion | flops 4194304 | bytes 6291456 | tf_op jit(solution)/shard_map/convert_element_type | solution.py:289
  8.8 3.2 %collective-permute-start.1 = (bf16[128,4096]{1,0:T(8,128)(2,1)S(1)}, bf16[128,4096]{1,0:T(8,128)(2,1)}, u32[]{:S(2)}, u32[]{:S(2)}) collective-permute-start(bf16[128,4096]{1,0:T(8,128)(2,1)S(1)} %get-tuple-element.9.cur_ref), channel_id=1, source_target_pairs={{0,1},{1,2},{2,3},{3,4},{4,5},{5,6},{6,7},{7,8},{8,9},{9,10},{10,1... | collective-permute-start | bytes 3145736 | tf_op jit(solution)/shard_map/ppermute | solution.py:291
  12.1 0.7 convert_reduce_fusion
  12.8 2.4 %stack.62.info_ref = s32[7]{0:T(128)} concatenate(s32[1]{0:T(128)} %bitcast.7, s32[1]{0:T(128)} %bitcast.1, s32[1]{0:T(128)} %bitcast.1, s32[1]{0:T(128)} %bitcast.8, s32[1]{0:T(128)} %bitcast.4, s32[1]{0:T(128)} %bitcast.5, s32[1]{0:T(128)} %bitcast.6), dimensions={0} | concatenate | bytes 56 | tf_op jit(solution)/shard_map/stack | solution.py:298
  15.3 7.5 %shard_map.95.refs_5_.refs_0_ = f32[512,640]{1,0:T(8,128)} custom-call(s32[7]{0:T(128)} %stack.62.info_ref, bf16[512,1024]{1,0:T(8,128)(2,1)} %refs_0_.5, bf16[512,1024]{1,0:T(8,128)(2,1)} %refs_1_.5, bf16[512,1024]{1,0:T(8,128)(2,1)} %refs_2_.5, bf16[512,1024]{1,0:T(8,128)(2,1)} %collective-permute-done.4.refs_3_.refs_4_, ...), custom_call_target="tpu_custom_call" | custom-call | flops 1048576 | bytes 1048576 | tf_op jit(solution)/shard_map/pallas_call | solution.py:194
  22.8 1.0 %copy-done = bf16[512,1024]{1,0:T(8,128)(2,1)} copy-done((bf16[512,1024]{1,0:T(8,128)(2,1)}, bf16[512,1024]{1,0:T(8,128)(2,1)S(1)}, u32[]{:S(2)}) %copy-start) | copy-done | bytes 1048600
  23.8 7.5 %shard_map.96.refs_5_.refs_2_ = f32[512,640]{1,0:T(8,128)} custom-call(s32[7]{0:T(128)} %stack.62.info_ref, bf16[512,1024]{1,0:T(8,128)(2,1)} %refs_0_.5, bf16[512,1024]{1,0:T(8,128)(2,1)} %refs_1_.5, bf16[512,1024]{1,0:T(8,128)(2,1)} %refs_2_.5, bf16[512,1024]{1,0:T(8,128)(2,1)} %copy-done, bf16[512,1024]{1,0:T(8,128)(2,1)} %copy-done, ...), custom_call_target="tpu_custom_call" | custom-call | flops 1048576 | bytes 1048576 | tf_op jit(solution)/shard_map/pallas_call | solution.py:194
  31.3 11.3 %collective-permute-done.2.refs_0_.refs_1_.refs_2_ = bf16[512,1024]{1,0:T(8,128)(2,1)S(1)} collective-permute-done((bf16[512,1024]{1,0:T(8,128)(2,1)}, bf16[512,1024]{1,0:T(8,128)(2,1)S(1)}, u32[]{:S(2)}, u32[]{:S(2)}) %collective-permute-start.2) | collective-permute-done | bytes 1048608 | tf_op jit(solution)/shard_map/ppermute | solution.py:276
  42.5 2.8 %collective-permute-start.5 = (bf16[512,1024]{1,0:T(8,128)(2,1)S(1)}, bf16[512,1024]{1,0:T(8,128)(2,1)S(1)}, u32[]{:S(2)}, u32[]{:S(2)}) collective-permute-start(bf16[512,1024]{1,0:T(8,128)(2,1)S(1)} %collective-permute-done.2.refs_0_.refs_1_.refs_2_), channel_id=1, source_target_pairs={{8,12},{12,8},{9,13},{13,9},{10,14},{14,10},{11,15},{15,11},{24,28... | collective-permute-start | bytes 3145736 | tf_op jit(solution)/shard_map/ppermute | solution.py:322
  45.3 1.9 %collective-permute-start = (bf16[128,4096]{1,0:T(8,128)(2,1)}, bf16[128,4096]{1,0:T(8,128)(2,1)}, u32[]{:S(2)}, u32[]{:S(2)}) collective-permute-start(bf16[128,4096]{1,0:T(8,128)(2,1)} %get-tuple-element.10.cur_ref), channel_id=1, source_target_pairs={{0,1},{1,2},{2,3},{3,4},{4,5},{5,6},{6,7},{7,8},{8,9},{9,10},{10,1... | collective-permute-start | bytes 3145736 | tf_op jit(solution)/shard_map/ppermute | solution.py:291
  47.3 2.5 %stack.65.info_ref = s32[7]{0:T(128)} concatenate(s32[1]{0:T(128)} %bitcast.9, s32[1]{0:T(128)} %bitcast.10, s32[1]{0:T(128)} %bitcast.1, s32[1]{0:T(128)} %bitcast.8, s32[1]{0:T(128)} %bitcast.4, s32[1]{0:T(128)} %bitcast.5, s32[1]{0:T(128)} %bitcast.6), dimensions={0} | concatenate | bytes 56 | tf_op jit(solution)/shard_map/stack | solution.py:298
  49.7 2.7 %shard_map.97.refs_5_ = bf16[512,640]{1,0:T(8,128)(2,1)} custom-call(s32[7]{0:T(128)} %stack.65.info_ref, bf16[512,1024]{1,0:T(8,128)(2,1)} %copy-done.2, bf16[512,1024]{1,0:T(8,128)(2,1)} %refs_1_.5, bf16[512,1024]{1,0:T(8,128)(2,1)} %refs_2_.5, bf16[512,1024]{1,0:T(8,128)(2,1)} %copy-done, bf16[512,1024]{1,0:T(8,128)(2,1)} %copy-done, ...), custom_call_target="tpu_custom_call" | custom-call | flops 1048576 | bytes 1048576 | tf_op jit(solution)/shard_map/pallas_call | solution.py:194
  52.4 1.3 %collective-permute-start.6 = (bf16[512,640]{1,0:T(8,128)(2,1)}, bf16[512,640]{1,0:T(8,128)(2,1)}, u32[]{:S(2)}, u32[]{:S(2)}) collective-permute-start(bf16[512,640]{1,0:T(8,128)(2,1)} %shard_map.97.refs_5_), channel_id=1, source_target_pairs={{0,8},{4,12},{1,9},{5,13},{2,10},{6,14},{3,11},{7,15},{16,24},{20,... | collective-permute-start | bytes 1966088 | tf_op jit(solution)/shard_map/ppermute | solution.py:331
  53.8 2.6 %stack.59.info_ref = s32[7]{0:T(128)} concatenate(s32[1]{0:T(128)} %bitcast, s32[1]{0:T(128)} %bitcast.1, s32[1]{0:T(128)} %bitcast.2, s32[1]{0:T(128)} %bitcast.3, s32[1]{0:T(128)} %bitcast.4, s32[1]{0:T(128)} %bitcast.5, s32[1]{0:T(128)} %bitcast.6), dimensions={0} | concatenate | bytes 56 | tf_op jit(solution)/shard_map/stack | solution.py:298
  56.4 0.7 fusion.4.mask_ref
  57.1 1.0 %copy-done.4 = bf16[512,1024]{1,0:T(8,128)(2,1)} copy-done((bf16[512,1024]{1,0:T(8,128)(2,1)}, bf16[512,1024]{1,0:T(8,128)(2,1)S(1)}, u32[]{:S(2)}) %copy-start.4) | copy-done | bytes 1048600
  58.1 7.5 %shard_map.98.rest_0_.refs_1_ = bf16[512,640]{1,0:T(8,128)(2,1)} custom-call(s32[7]{0:T(128)} %stack.59.info_ref, bf16[512,1024]{1,0:T(8,128)(2,1)} %refs_0_.5, bf16[512,1024]{1,0:T(8,128)(2,1)} %copy-done.2, bf16[512,1024]{1,0:T(8,128)(2,1)} %copy-done.2, bf16[512,1024]{1,0:T(8,128)(2,1)} %copy-done.4, bf16[512,1024]{1,0:T(8,128)(2,1)} %copy-done.4, ...), custom_call_target="tpu_custom_call" | custom-call | flops 1048576 | bytes 1048576 | tf_op jit(solution)/shard_map/pallas_call | solution.py:194
  65.6 9.5 %shard_map.99.rest_0_ = bf16[128,8192]{1,0:T(8,128)(2,1)} custom-call(bf16[512,128]{1,0:T(8,128)(2,1)} %filt_ref.3, bf16[256,128]{1,0:T(8,128)(2,1)} %fusion.4.mask_ref, bf16[128,4096]{1,0:T(8,128)(2,1)} %collective-permute-done.1.refs_6_.prev_ref, bf16[128,4096]{1,0:T(8,128)(2,1)} %copy-done.3, bf16[128,8192]{1,0:T(8,128)(2,1)} %gate_ref.3, ...), custom_call_target="tpu_custom_call" | custom-call | flops 1048576 | bytes 1048576 | tf_op jit(solution)/shard_map/pallas_call | solution.py:72
  75.1 9.5 %shard_map.100.refs_4_ = bf16[128,8192]{1,0:T(8,128)(2,1)} custom-call(bf16[512,128]{1,0:T(8,128)(2,1)} %filt_ref.3, bf16[256,128]{1,0:T(8,128)(2,1)} %fusion.4.mask_ref, bf16[128,4096]{1,0:T(8,128)(2,1)} %collective-permute-done.prev_ref, bf16[128,4096]{1,0:T(8,128)(2,1)} %get-tuple-element.10.cur_ref, ...), custom_call_target="tpu_custom_call", output_to_operand_aliasing={{}: (5, {})} | custom-call | flops 1048576 | bytes 1048576 | tf_op jit(solution)/shard_map/pallas_call | solution.py:72
  84.6 4.1 %shard_map.101 = bf16[512,1024]{1,0:T(8,128)(2,1)} custom-call(s32[1]{0:T(128)} %bitcast.11.has_ref, f32[512,640]{1,0:T(8,128)} %shard_map.95.refs_5_.refs_0_, bf16[512,640]{1,0:T(8,128)(2,1)} %shard_map.98.rest_0_.refs_1_, f32[512,640]{1,0:T(8,128)} %shard_map.96.refs_5_.refs_2_, bf16[512,640]{1,0:T(8,128)(2,1)} %collective-permute-done.6.refs_3_, ...), custom_call_target="tpu_custom_call" | custom-call | flops 1048576 | bytes 1048576 | tf_op jit(solution)/shard_map/pallas_call | solution.py:249
  (25 shorter events, 1.3 us)
Async XLA Ops:
  2.3 1.8 %copy-start.1 = (bf16[512,1024]{1,0:T(8,128)(2,1)S(1)}, bf16[512,1024]{1,0:T(8,128)(2,1)}, u32[]{:S(2)}) copy-start(bf16[512,1024]{1,0:T(8,128)(2,1)} %refs_0_.5) | copy-start | bytes 3145732
  3.4 19.4 %collective-permute-start.3 = (bf16[512,1024]{1,0:T(8,128)(2,1)}, bf16[512,1024]{1,0:T(8,128)(2,1)S(1)}, u32[]{:S(2)}, u32[]{:S(2)}) collective-permute-start(bf16[512,1024]{1,0:T(8,128)(2,1)} %pad_maximum_fusion.1), channel_id=1, source_target_pairs={{0,4},{4,0},{8,12},{12,8},{1,5},{5,1},{9,13},{13,9},{2,6},{6,2},{1... | collective-permute-start | bytes 3145736 | tf_op jit(solution)/shard_map/ppermute | solution.py:278
  4.1 2.5 %copy-start.5 = (bf16[128,8192]{1,0:T(8,128)(2,1)S(1)}, bf16[128,8192]{1,0:T(8,128)(2,1)}, u32[]{:S(2)}) copy-start(bf16[128,8192]{1,0:T(8,128)(2,1)} %param.10) | copy-start | bytes 6291460
  4.1 3.0 %copy-start.6 = (bf16[128,8192]{1,0:T(8,128)(2,1)S(1)}, bf16[128,8192]{1,0:T(8,128)(2,1)}, u32[]{:S(2)}) copy-start(bf16[128,8192]{1,0:T(8,128)(2,1)} %param.9) | copy-start | bytes 6291460
  5.9 9.3 %collective-permute-start.4 = (bf16[512,1024]{1,0:T(8,128)(2,1)}, bf16[512,1024]{1,0:T(8,128)(2,1)}, u32[]{:S(2)}, u32[]{:S(2)}) collective-permute-start(bf16[512,1024]{1,0:T(8,128)(2,1)} %get-tuple-element.11), channel_id=1, source_target_pairs={{0,4},{4,0},{8,12},{12,8},{1,5},{5,1},{9,13},{13,9},{2,6},{6,2},{1... | collective-permute-start | bytes 3145736 | tf_op jit(solution)/shard_map/ppermute | solution.py:277
  6.4 5.7 %copy-start.7 = (s32[2048]{0:T(1024)S(1)}, s32[2048]{0:T(1024)}, u32[]{:S(2)}) copy-start(s32[2048]{0:T(1024)} %param.12) | copy-start | bytes 24580
  6.4 36.2 %collective-permute-start.2 = (bf16[512,1024]{1,0:T(8,128)(2,1)}, bf16[512,1024]{1,0:T(8,128)(2,1)S(1)}, u32[]{:S(2)}, u32[]{:S(2)}) collective-permute-start(bf16[512,1024]{1,0:T(8,128)(2,1)} %get-tuple-element.12), channel_id=1, source_target_pairs={{0,8},{4,12},{8,0},{12,4},{1,9},{5,13},{9,1},{13,5},{2,10},{6,14},... | collective-permute-start | bytes 3145736 | tf_op jit(solution)/shard_map/ppermute | solution.py:276
  8.8 13.9 %copy-start.3 = (bf16[128,4096]{1,0:T(8,128)(2,1)}, bf16[128,4096]{1,0:T(8,128)(2,1)S(1)}, u32[]{:S(2)}) copy-start(bf16[128,4096]{1,0:T(8,128)(2,1)S(1)} %get-tuple-element.9.cur_ref) | copy-start | bytes 3145732
  8.8 48.3 %collective-permute-start.1 = (bf16[128,4096]{1,0:T(8,128)(2,1)S(1)}, bf16[128,4096]{1,0:T(8,128)(2,1)}, u32[]{:S(2)}, u32[]{:S(2)}) collective-permute-start(bf16[128,4096]{1,0:T(8,128)(2,1)S(1)} %get-tuple-element.9.cur_ref), channel_id=1, source_target_pairs={{0,1},{1,2},{2,3},{3,4},{4,5},{5,6},{6,7},{7,8},{8,9},{9,10},{10,1... | collective-permute-start | bytes 3145736 | tf_op jit(solution)/shard_map/ppermute | solution.py:291
  22.8 1.0 %copy-start = (bf16[512,1024]{1,0:T(8,128)(2,1)}, bf16[512,1024]{1,0:T(8,128)(2,1)S(1)}, u32[]{:S(2)}) copy-start(bf16[512,1024]{1,0:T(8,128)(2,1)S(1)} %collective-permute-done.3.refs_3_.refs_4_) | copy-start | bytes 3145732
  42.5 7.2 %copy-start.2 = (bf16[512,1024]{1,0:T(8,128)(2,1)}, bf16[512,1024]{1,0:T(8,128)(2,1)S(1)}, u32[]{:S(2)}) copy-start(bf16[512,1024]{1,0:T(8,128)(2,1)S(1)} %collective-permute-done.2.refs_0_.refs_1_.refs_2_) | copy-start | bytes 3145732
  42.5 14.6 %collective-permute-start.5 = (bf16[512,1024]{1,0:T(8,128)(2,1)S(1)}, bf16[512,1024]{1,0:T(8,128)(2,1)S(1)}, u32[]{:S(2)}, u32[]{:S(2)}) collective-permute-start(bf16[512,1024]{1,0:T(8,128)(2,1)S(1)} %collective-permute-done.2.refs_0_.refs_1_.refs_2_), channel_id=1, source_target_pairs={{8,12},{12,8},{9,13},{13,9},{10,14},{14,10},{11,15},{15,11},{24,28... | collective-permute-start | bytes 3145736 | tf_op jit(solution)/shard_map/ppermute | solution.py:322
  45.3 29.8 %collective-permute-start = (bf16[128,4096]{1,0:T(8,128)(2,1)}, bf16[128,4096]{1,0:T(8,128)(2,1)}, u32[]{:S(2)}, u32[]{:S(2)}) collective-permute-start(bf16[128,4096]{1,0:T(8,128)(2,1)} %get-tuple-element.10.cur_ref), channel_id=1, source_target_pairs={{0,1},{1,2},{2,3},{3,4},{4,5},{5,6},{6,7},{7,8},{8,9},{9,10},{10,1... | collective-permute-start | bytes 3145736 | tf_op jit(solution)/shard_map/ppermute | solution.py:291
  52.4 32.2 %collective-permute-start.6 = (bf16[512,640]{1,0:T(8,128)(2,1)}, bf16[512,640]{1,0:T(8,128)(2,1)}, u32[]{:S(2)}, u32[]{:S(2)}) collective-permute-start(bf16[512,640]{1,0:T(8,128)(2,1)} %shard_map.97.refs_5_), channel_id=1, source_target_pairs={{0,8},{4,12},{1,9},{5,13},{2,10},{6,14},{3,11},{7,15},{16,24},{20,... | collective-permute-start | bytes 1966088 | tf_op jit(solution)/shard_map/ppermute | solution.py:331
  57.1 1.0 %copy-start.4 = (bf16[512,1024]{1,0:T(8,128)(2,1)}, bf16[512,1024]{1,0:T(8,128)(2,1)S(1)}, u32[]{:S(2)}) copy-start(bf16[512,1024]{1,0:T(8,128)(2,1)S(1)} %collective-permute-done.5.refs_3_.refs_4_) | copy-start | bytes 3145732
